TPU v7x, 1024 devices: a whole 8x8x8 slice. The times are simulated.
1024 devices in a mesh: row: 32 (over z, y_hi, core), col: 32 (over y_lo, x).
Axes of the slice: x: 8, y: 8 (y_hi: 2, y_lo: 4; y = y_hi * 4 + y_lo), z: 8, core: 2. Of those that a mesh axis runs over, the one named last changes fastest.
Arguments:
- grad: bfloat16 [8192, 4096], P('row', 'col'), may hold values from -6 to 6
- basis_t: bfloat16 [8192, 8192], P('row', 'col'), may hold values from -0.125 to 0.125
- first_moment: float32 [8192, 4096], P('row', 'col'), may hold values from -4 to 4
- second_moment: float32 [8192, 4096], P('row', 'col'), may hold values from 0.1 to 3
- master: float32 [8192, 4096], P('row', 'col'), may hold values from -6 to 6
Outputs:
- new_first: float32 [8192, 4096], P('row', 'col')
- new_second: float32 [8192, 4096], P('row', 'col')
- new_master: float32 [8192, 4096], P('row', 'col')
- new_weight: bfloat16 [8192, 4096], P('row', 'col')
- rotated_back: float32 [8192, 4096], P('row', 'col')
All inputs are finite; a program needn't handle non-finite values.
Results may differ from a plain program's by a relative error of at most 0.019.
Values may be sent and summed in bfloat16 or wider, within the bound.
A program may use at most 32 MiB of HBM per device.

v0:
```python
import jax
import jax.numpy as jnp
from jax import lax
from jax.sharding import PartitionSpec as P

STEP = 10


BETA_ONE = 0.9
BETA_TWO = 0.95
EPSILON = 1e-08
LEARN = 0.01
DECAY = 0.1


def shards(grad, basis_t, first_moment, second_moment, master):
    tall = lax.all_gather(grad, "row", axis=0, tiled=True)
    wide = lax.all_gather(basis_t, "col", axis=1, tiled=True)
    rotated = jnp.dot(wide, tall, preferred_element_type=jnp.float32)
    new_first = BETA_ONE * first_moment + (1.0 - BETA_ONE) * rotated
    new_second = BETA_TWO * second_moment + (1.0 - BETA_TWO) * rotated * rotated
    corr_one = 1.0 - BETA_ONE**STEP
    corr_two = 1.0 - BETA_TWO**STEP
    direction = (new_first / corr_one / (jnp.sqrt(new_second / corr_two) + EPSILON)).astype(
        jnp.bfloat16
    )
    terms = lax.dot_general(
        wide, direction, (((0,), (0,)), ((), ())), preferred_element_type=jnp.float32
    )
    rotated_back = lax.psum_scatter(
        terms.astype(jnp.bfloat16), "row", scatter_dimension=0, tiled=True
    ).astype(jnp.float32)
    new_master = master * (1.0 - LEARN * DECAY) - LEARN * rotated_back
    new_weight = new_master.astype(jnp.bfloat16)
    return (new_first, new_second, new_master, new_weight, rotated_back)


def solution(mesh):
    placed = (P("row", "col"), P("row", "col"), P("row", "col"), P("row", "col"), P("row", "col"))
    return jax.shard_map(
        shards,
        mesh=mesh,
        in_specs=placed,
        out_specs=(
            P("row", "col"),
            P("row", "col"),
            P("row", "col"),
            P("row", "col"),
            P("row", "col"),
        ),
        check_vma=False,
    )
```

profile of v0, /device:TPU:1, one launch (start us, length us, event | category | flops | bytes accessed | tf_op | source)
XLA Modules:
  0.0 420.5 jit_solution(11586357592346242773)
XLA Ops:
  7.2 0.0 all-gather.5.cloned.1.call-start
  7.2 0.7 all-gather.5.cloned.1.call-update
  7.9 0.0 all-gather.3.cloned.1.call-start
  7.9 0.7 all-gather.3.cloned.1.call-update
  8.7 0.0 reduce-scatter.2.cloned.1.call-start
  8.7 117.7 %all-gather.5.cloned.1.call-done = bf16[8192,128]{1,0:T(8,128)(2,1)} async-done(((bf16[256,128]{1,0:T(8,128)(2,1)}), bf16[8192,128]{1,0:T(8,128)(2,1)}) %all-gather.5.cloned.1.call-update) | async-done | bytes 2097168 | tf_op jit(solution)/shard_map/all_gather | solution.py:17
  126.4 119.6 %all-gather.3.cloned.1.call-done = bf16[256,8192]{1,0:T(8,128)(2,1)} async-done(((bf16[256,256]{1,0:T(8,128)(2,1)}), bf16[256,8192]{1,0:T(8,128)(2,1)}) %all-gather.3.cloned.1.call-update) | async-done | bytes 4194320 | tf_op jit(solution)/shard_map/all_gather | solution.py:18
  246.0 0.0 copy-start
  246.0 4.2 %fusion.1 = (f32[256,128]{1,0:T(8,128)S(1)}, f32[256,128]{1,0:T(8,128)S(1)}) fusion(f32[256,128]{1,0:T(8,128)} %param.8, f32[256,128]{1,0:T(8,128)} %param.7, bf16[256,8192]{1,0:T(8,128)(2,1)} %all-gather.3.cloned.1.call-done, bf16[8192,128]{1,0:T(8,128)(2,1)} %all-gather.5.cloned.1.call-done), kind=kOutput, calls=%fused_computation.3 | convolution fusion | flops 537100288 | bytes 6815744 | tf_op jit(solution)/shard_map/dot_general | solution.py:19
  250.2 0.0 copy-start.1
  250.3 0.0 copy-start.2
  250.3 0.0 copy-done
  250.3 0.0 copy-start.3
  250.3 2.1 fusion
  252.4 0.0 reduce-scatter.2.cloned.1.call-update
  252.4 0.0 copy-done.1
  252.5 0.0 copy-done.2
  252.5 0.0 copy-done.3
  252.5 0.1 copy.10
  252.6 157.4 %reduce-scatter.2.cloned.1.call-done = bf16[256,128]{0,1:T(8,128)(2,1)} async-done(((bf16[8192,128]{0,1:T(8,128)(2,1)}), bf16[256,128]{0,1:T(8,128)(2,1)}) %reduce-scatter.2.cloned.1.call-update) | async-done | bytes 65552 | tf_op jit(solution)/shard_map/reduce_scatter | solution.py:30
  410.0 0.9 fusion.8
  410.9 0.7 copy.12
  411.6 0.8 copy.11
  412.4 1.6 copy.13
Async XLA Ops:
  7.2 119.2 %all-gather.5.cloned.1.call-start = ((), (), s32[]{:S(2)}) async-start(), calls=%async_computation.2 | async-start | bytes 2162688 | tf_op jit(solution)/shard_map/all_gather | solution.py:17
  7.9 238.1 %all-gather.3.cloned.1.call-start = ((), (), s32[]{:S(2)}) async-start(), calls=%async_computation.1 | async-start | bytes 4325376 | tf_op jit(solution)/shard_map/all_gather | solution.py:18
  8.7 401.4 %reduce-scatter.2.cloned.1.call-start = ((), (), s32[]{:S(2)}) async-start(), calls=%async_computation.3 | async-start | bytes 2162688 | tf_op jit(solution)/shard_map/reduce_scatter | solution.py:30
  246.0 4.3 %copy-start = (bf16[256,8192]{1,0:T(8,128)(2,1)S(1)}, bf16[256,8192]{1,0:T(8,128)(2,1)}, u32[]{:S(2)}) copy-start(bf16[256,8192]{1,0:T(8,128)(2,1)} %all-gather.3.cloned.1.call-done) | copy-start | bytes 12582916
  250.2 2.2 copy-start.1
  250.3 2.2 copy-start.2
  250.3 2.2 copy-start.3
Sparse Core Ops, SparseCore 0:
  12.5 113.8 all-gather.4
  129.0 116.9 all-gather.2
  252.6 157.4 reduce-scatter.1
where the time goes:
time: 425 us; the launch traced here: 421 us
  waiting for transfers between devices  396 us (93%)
  between operations  13.8 us (3%)
  matrix products  6.34 us (1%)
    reduce_scatter x1, waiting for transfers between devices, shards(): lax.psum_scatter(terms.astype(jnp.bfloat16), 'row', scatter_dimension=0,...  157 us
    all_gather x1, waiting for transfers between devices, shards(): wide = lax.all_gather(basis_t, 'col', axis=1, tiled=True)  120 us
    all_gather x1, waiting for transfers between devices, shards(): tall = lax.all_gather(grad, 'row', axis=0, tiled=True)  118 us
  transfers between devices with their start and end apart: 3, of which 3 were waited for; matrix products, arithmetic and copies ran while one was open for 0% of the time, Pallas kernels for 0%

commit v1 on v0

v1 whole, which is shorter than its diff:
```python
import jax
import jax.numpy as jnp
from jax import lax
from jax.experimental import pallas as pl
from jax.experimental.pallas import tpu as pltpu
from jax.sharding import PartitionSpec as P

STEP = 10
BETA_ONE = 0.9
BETA_TWO = 0.95
EPSILON = 1e-08
LEARN = 0.01
DECAY = 0.1

MESH = pl.DeviceIdType.MESH
F32 = jnp.float32
BF16 = jnp.bfloat16

RIGHT = (4, 3, 3, 4)
LEFT = (3, 4, 4, 3)
Z_RIGHT = (4, 3)
Z_LEFT = (3, 4)
DELTAS = (4, 3, -3, 2, -2, 1, -1, 0)


def kernel(
    g_ref, b_ref, fm_ref, sm_ref, ma_ref,
    nf_ref, ns_ref, nm_ref, nw_ref, rb_ref,
    stage, wide, tall, acc, part_out, part_in, turned,
    own, core_out, core_in, ring_out, ring_in, last_out, last_in,
    y_s, y_r, x_s, x_r, g_s, g_r, z_s, z_r, gc_s, gc_r, p_s, p_r, tc_s, tc_r, r_s, r_r, f_s, f_r,
):
    row, col = lax.axis_index("row"), lax.axis_index("col")
    z, yh, c = row // 4, (row // 2) % 2, row % 2
    yl, x = col // 8, col % 8
    h = yl % 2
    mate = yl + 1 - 2 * h
    far = 1 - yh

    def at(z_, yh_, c_, yl_, x_):
        return (z_ * 4 + yh_ * 2 + c_, yl_ * 8 + x_)

    right, left = at(z, yh, c, yl, (x + 1) % 8), at(z, yh, c, yl, (x + 7) % 8)
    above, below = at((z + 1) % 8, yh, c, yl, x), at((z + 7) % 8, yh, c, yl, x)
    twin = at(z, yh, 1 - c, yl, x)
    pair = at(z, yh, c, mate, x)
    across = at(z, far, c, yl, x)
    across_pair = at(z, far, c, mate, x)

    waits = []

    def copy(src, dst, send, recv, to):
        made = pltpu.make_async_remote_copy(
            src_ref=src, dst_ref=dst, send_sem=send, recv_sem=recv, device_id=to, device_id_type=MESH
        )
        made.start()
        waits.append(made)

    def arrived(dst, send, recv, frm):
        pltpu.make_async_remote_copy(
            src_ref=dst, dst_ref=dst, send_sem=send, recv_sem=recv, device_id=frm, device_id_type=MESH
        ).wait_recv()

    here = yl * 8 + x
    stage[0] = b_ref[:, 0:128]
    stage[1] = b_ref[:, 128:256]
    wide[here] = stage[h]
    tall[z, c, yh, 0] = g_ref[pl.ds(pl.multiple_of(h * 128, 128), 128), :]

    barrier = pltpu.get_barrier_semaphore()
    peers = [right, left, above, below, twin, across, across_pair]
    peers += [at(z, yh, c, (yl + d) % 4, x) for d in (1, 2, 3)]
    for peer in peers:
        pl.semaphore_signal(barrier, inc=1, device_id=peer, device_id_type=MESH)
    pl.semaphore_wait(barrier, len(peers))

    def x_step(d, s):
        line = ((yl + 4 - d) % 4) * 8
        for way, count, sign, to in ((0, RIGHT[d], -1, right), (1, LEFT[d], 1, left)):
            if s >= count:
                continue
            slot = wide.at[line + (x + 8 + sign * s) % 8]
            if s:
                arrived(slot, x_s.at[way, d, s - 1], x_r.at[way, d, s - 1], to)
            copy(slot, slot, x_s.at[way, d, s], x_r.at[way, d, s], to)

    def x_last(d, way):
        line = ((yl + 4 - d) % 4) * 8
        count, sign, to = ((RIGHT[d], -1, right), (LEFT[d], 1, left))[way]
        slot = wide.at[line + (x + 8 + sign * count) % 8]
        arrived(slot, x_s.at[way, d, count - 1], x_r.at[way, d, count - 1], to)

    def y_arrived(d):
        arrived(wide.at[((yl + 4 - d) % 4) * 8 + x], y_s.at[d - 1], y_r.at[d - 1], pair)

    halves = (yh, far)

    def to_twin(a, way, s):
        sign = (-1, 1)[way]
        slot = tall.at[(z + 8 + sign * s) % 8, c, halves[a]]
        copy(slot, slot, gc_s.at[way, a, s], gc_r.at[way, a, s], twin)

    def twin_arrived(a, way, s):
        sign = (-1, 1)[way]
        slot = tall.at[(z + 8 + sign * s) % 8, 1 - c, halves[a]]
        arrived(slot, gc_s.at[way, a, s], gc_r.at[way, a, s], twin)

    def z_step(a, s):
        for way, count, sign, to in ((0, Z_RIGHT[a], -1, above), (1, Z_LEFT[a], 1, below)):
            if s > count:
                continue
            slot = tall.at[(z + 8 + sign * s) % 8, c, halves[a]]
            if s:
                arrived(slot, z_s.at[way, a, s - 1], z_r.at[way, a, s - 1], to)
            if s < count:
                copy(slot, slot, z_s.at[way, a, s], z_r.at[way, a, s], to)
            if s or way == 0:
                to_twin(a, way, s)

    x_step(0, 0)
    keep = g_ref.at[pl.ds(pl.multiple_of(h * 128, 128), 128), :]
    give = g_ref.at[pl.ds(pl.multiple_of((1 - h) * 128, 128), 128), :]
    copy(give, tall.at[z, c, yh, 1], g_s.at[1], g_r.at[1], pair)
    copy(keep, tall.at[z, c, yh, 0], g_s.at[0], g_r.at[0], across)
    copy(give, tall.at[z, c, yh, 1], g_s.at[2], g_r.at[2], across_pair)
    for d in (1, 3, 2):
        there = (yl + d) % 4
        copy(stage.at[there % 2], wide.at[here], y_s.at[d - 1], y_r.at[d - 1], at(z, yh, c, there, x))

    arrived(tall.at[z, c, yh, 1], g_s.at[1], g_r.at[1], pair)
    z_step(0, 0)
    x_step(0, 1)
    y_arrived(1)
    x_step(1, 0)
    y_arrived(3)
    x_step(3, 0)
    arrived(tall.at[z, c, far, 0], g_s.at[0], g_r.at[0], across)
    arrived(tall.at[z, c, far, 1], g_s.at[2], g_r.at[2], across_pair)
    z_step(1, 0)
    z_step(0, 1)
    x_step(0, 2)
    y_arrived(2)
    x_step(2, 0)
    x_step(1, 1)
    x_step(3, 1)
    z_step(1, 1)
    z_step(0, 2)
    x_step(0, 3)
    x_step(2, 1)
    x_step(1, 2)
    x_step(3, 2)
    z_step(1, 2)
    z_step(0, 3)
    x_step(2, 2)
    x_step(1, 3)
    x_step(3, 3)
    z_step(1, 3)
    x_step(2, 3)
    z_step(0, 4)
    z_step(1, 4)
    for s in range(5):
        for a in (0, 1):
            for way, count in ((0, Z_RIGHT[a]), (1, Z_LEFT[a])):
                if s <= count and (s or way == 0):
                    twin_arrived(a, way, s)
    for d in range(4):
        x_last(d, 0 if RIGHT[d] == 3 else 1)

    def operands(delta):
        xs = (x + 8 + delta) % 8
        lhs = jnp.concatenate([wide[line * 8 + xs] for line in range(4)], axis=1)

        def rhs(e):
            return jnp.concatenate(
                [tall[line * 2 + xs // 4, xs % 2, (xs // 2) % 2, e] for line in range(4)], axis=0
            )

        return lhs, rhs

    for i, delta in enumerate((0, 1, -1, 2, -2, 3, -3)):
        lhs, rhs = operands(delta)
        for e in (0, 1):
            term = jnp.dot(lhs, rhs(e), preferred_element_type=F32)
            acc[e] = term if i == 0 else acc[e] + term
    for d in range(4):
        x_last(d, 0 if RIGHT[d] == 4 else 1)
    lhs, rhs = operands(4)
    part_out[...] = (acc[1] + jnp.dot(lhs, rhs(1), preferred_element_type=F32)).astype(BF16)
    copy(part_out, part_in, p_s.at[0], p_r.at[0], pair)
    acc[0] = acc[0] + jnp.dot(lhs, rhs(0), preferred_element_type=F32)
    arrived(part_in, p_s.at[0], p_r.at[0], pair)

    rotated = acc[0] + part_in[...].astype(F32)
    new_first = BETA_ONE * fm_ref[...] + (1.0 - BETA_ONE) * rotated
    new_second = BETA_TWO * sm_ref[...] + (1.0 - BETA_TWO) * rotated * rotated
    nf_ref[...] = new_first
    ns_ref[...] = new_second
    corr_one = 1.0 - BETA_ONE**STEP
    corr_two = 1.0 - BETA_TWO**STEP
    direction = new_first / corr_one / (jnp.sqrt(new_second / corr_two) + EPSILON)
    turned[0] = direction.T.astype(BF16)
    copy(turned.at[0], turned.at[1], p_s.at[1], p_r.at[1], pair)

    def terms(e):
        lhs = turned[e]
        for i, delta in enumerate(DELTAS):
            base = ((z + 8 + delta) % 8) * 4
            for half in (0, 1):
                rhs = jnp.concatenate([wide[base + half * 2 + c], wide[base + half * 2 + 1 - c]], axis=1)
                term = jnp.dot(lhs, rhs, preferred_element_type=F32)
                own[e, i, half] = term[:, 0:128]
                core_out[e, i, half] = term[:, 128:256].astype(BF16)
            copy(core_out.at[e, i], core_in.at[e, i], tc_s.at[e, i], tc_r.at[e, i], twin)

    def z_ring(e, t):
        for way, to in ((0, above), (1, below)):
            i = DELTAS.index((4 - t) if way == 0 or t == 0 else t - 4)
            if t or way == 0:
                arrived(core_in.at[e, i], tc_s.at[e, i], tc_r.at[e, i], twin)
            if t == 0:
                some = ring_out.at[way, e, 0, way]
                some[...] = (own[e, i, way] + core_in[e, i, way].astype(F32)).astype(BF16)
                copy(some, ring_in.at[way, e, 0, way], r_s.at[way, e, 0], r_r.at[way, e, 0], to)
                continue
            if t == 1:
                came = ring_in.at[way, e, 0, way]
                arrived(came, r_s.at[way, e, 0], r_r.at[way, e, 0], to)
                for half in (0, 1):
                    total = own[e, i, half] + core_in[e, i, half].astype(F32)
                    if half == way:
                        total += came[...].astype(F32)
                    ring_out[way, e, t, half] = total.astype(BF16)
            else:
                came = ring_in.at[way, e, t - 1]
                arrived(came, r_s.at[way, e, t - 1], r_r.at[way, e, t - 1], to)
                total = own[e, i] + core_in[e, i].astype(F32) + came[...].astype(F32)
                ring_out[way, e, t] = total.astype(BF16)
            copy(ring_out.at[way, e, t], ring_in.at[way, e, t], r_s.at[way, e, t], r_r.at[way, e, t], to)

    def z_sum(e):
        i = DELTAS.index(0)
        arrived(core_in.at[e, i], tc_s.at[e, i], tc_r.at[e, i], twin)
        for way, to in ((0, above), (1, below)):
            arrived(ring_in.at[way, e, 3], r_s.at[way, e, 3], r_r.at[way, e, 3], to)
        total = own[e, i] + core_in[e, i].astype(F32)
        total += ring_in[0, e, 3].astype(F32) + ring_in[1, e, 3].astype(F32)
        own[e, i] = total
        last_out[e] = total.astype(BF16)

    terms(0)
    z_ring(0, 0)
    arrived(turned.at[1], p_s.at[1], p_r.at[1], pair)
    terms(1)
    z_ring(1, 0)
    for t in (1, 2, 3):
        for e in (0, 1):
            z_ring(e, t)
    z_sum(0)
    copy(last_out.at[0, far], last_in.at[0], f_s.at[0], f_r.at[0], across)
    z_sum(1)
    copy(last_out.at[1, far], last_in.at[2], f_s.at[2], f_r.at[2], across_pair)
    copy(last_out.at[1, yh], last_in.at[1], f_s.at[1], f_r.at[1], pair)

    def finish(rows, value):
        back = value.T
        rb_ref[rows, :] = back
        new_master = ma_ref[rows, :] * (1.0 - LEARN * DECAY) - LEARN * back
        nm_ref[rows, :] = new_master
        nw_ref[rows, :] = new_master.astype(BF16)

    arrived(last_in.at[0], f_s.at[0], f_r.at[0], across)
    finish(
        pl.ds(pl.multiple_of(h * 128, 128), 128),
        own[0, DELTAS.index(0), yh] + last_in[0].astype(F32),
    )
    arrived(last_in.at[1], f_s.at[1], f_r.at[1], pair)
    arrived(last_in.at[2], f_s.at[2], f_r.at[2], across_pair)
    finish(
        pl.ds(pl.multiple_of((1 - h) * 128, 128), 128),
        last_in[1].astype(F32) + last_in[2].astype(F32),
    )
    for made in waits:
        made.wait_send()


def shards(grad, basis_t, first_moment, second_moment, master):
    rows, cols = grad.shape
    block = jax.ShapeDtypeStruct((rows, cols), F32)
    dma = pltpu.SemaphoreType.DMA
    return tuple(pl.pallas_call(
        kernel,
        out_shape=(block, block, block, jax.ShapeDtypeStruct((rows, cols), BF16), block),
        in_specs=[pl.BlockSpec(memory_space=pltpu.VMEM)] * 5,
        out_specs=tuple([pl.BlockSpec(memory_space=pltpu.VMEM)] * 5),
        scratch_shapes=[
            pltpu.VMEM((2, 256, 128), BF16),
            pltpu.VMEM((32, 256, 128), BF16),
            pltpu.VMEM((8, 2, 2, 2, 128, 128), BF16),
            pltpu.VMEM((2, 256, 128), F32),
            pltpu.VMEM((256, 128), BF16),
            pltpu.VMEM((256, 128), BF16),
            pltpu.VMEM((2, 128, 256), BF16),
            pltpu.VMEM((2, 8, 2, 128, 128), F32),
            pltpu.VMEM((2, 8, 2, 128, 128), BF16),
            pltpu.VMEM((2, 8, 2, 128, 128), BF16),
            pltpu.VMEM((2, 2, 4, 2, 128, 128), BF16),
            pltpu.VMEM((2, 2, 4, 2, 128, 128), BF16),
            pltpu.VMEM((2, 2, 128, 128), BF16),
            pltpu.VMEM((3, 128, 128), BF16),
            dma((3,)), dma((3,)),
            dma((2, 4, 4)), dma((2, 4, 4)),
            dma((3,)), dma((3,)),
            dma((2, 2, 4)), dma((2, 2, 4)),
            dma((2, 2, 5)), dma((2, 2, 5)),
            dma((2,)), dma((2,)),
            dma((2, 8)), dma((2, 8)),
            dma((2, 2, 4)), dma((2, 2, 4)),
            dma((3,)), dma((3,)),
        ],
        compiler_params=pltpu.CompilerParams(
            collective_id=0, has_side_effects=True, vmem_limit_bytes=40 * 2**20
        ),
        cost_estimate=pl.CostEstimate(flops=2 * 2 * 256 * 8192 * 128, bytes_accessed=2**20, transcendentals=0),
    )(grad, basis_t, first_moment, second_moment, master))


def solution(mesh):
    placed = tuple([P("row", "col")] * 5)
    return jax.shard_map(shards, mesh=mesh, in_specs=placed, out_specs=placed, check_vma=False)
```

time: 425 us -> 87 us (0.20)
  the two profiles are of different devices: /device:TPU:1 before, /device:TPU:16 now
where the time goes in v1:
time: 87 us; the launch traced here: 86.7 us
  Pallas kernels  78.4 us (90%)
  local copies, waits for them, and re-layouts  7.7 us (9%)
    pallas_call x1, Pallas kernels, shards(): pl.pallas_call(kernel, out_shape=(block, block, block, jax.ShapeDtypeStru...  78.4 us
    unnamed x15, local copies, waits for them, and re-layouts  7.7 us

profile of v1, /device:TPU:16, one launch (start us, length us, event | category | flops | bytes accessed | tf_op | source)
XLA Modules:
  0.0 86.7 jit_solution(5318604356644074166)
XLA Ops:
  0.6 0.0 copy-start
  0.6 0.9 %copy-done = bf16[256,256]{1,0:T(8,128)(2,1)S(1)} copy-done((bf16[256,256]{1,0:T(8,128)(2,1)S(1)}, bf16[256,256]{1,0:T(8,128)(2,1)}, u32[]{:S(2)}) %copy-start) | copy-done | bytes 131096
  1.5 0.0 copy-start.1
  1.5 0.9 %copy-done.1 = f32[256,128]{1,0:T(8,128)S(1)} copy-done((f32[256,128]{1,0:T(8,128)S(1)}, f32[256,128]{1,0:T(8,128)}, u32[]{:S(2)}) %copy-start.1) | copy-done | bytes 131096
  2.4 0.0 copy-start.2
  2.4 0.9 %copy-done.2 = f32[256,128]{1,0:T(8,128)S(1)} copy-done((f32[256,128]{1,0:T(8,128)S(1)}, f32[256,128]{1,0:T(8,128)}, u32[]{:S(2)}) %copy-start.2) | copy-done | bytes 131096
  3.3 0.0 copy-start.3
  3.3 0.9 %copy-done.3 = f32[256,128]{1,0:T(8,128)S(1)} copy-done((f32[256,128]{1,0:T(8,128)S(1)}, f32[256,128]{1,0:T(8,128)}, u32[]{:S(2)}) %copy-start.3) | copy-done | bytes 131096
  4.3 0.0 copy-start.4
  4.3 0.8 copy-done.4
  5.1 78.4 %shard_map.92 = (f32[256,128]{1,0:T(8,128)S(1)}, f32[256,128]{1,0:T(8,128)S(1)}, f32[256,128]{1,0:T(8,128)S(1)}, bf16[256,128]{1,0:T(8,128)(2,1)S(1)}, f32[256,128]{1,0:T(8,128)S(1)}) custom-call(bf16[256,128]{1,0:T(8,128)(2,1)S(1)} %copy-done.4, bf16[256,256]{1,0:T(8,128)(2,1)S(1)} %copy-done, f32[256,128]{1,0:T(8,128)S(1)} %copy-done.1, ...), custom_call_target="tpu_custom_call" | custom-call | flops 1073741824 | bytes 1048576 | tf_op jit(solution)/shard_map/pallas_call | solution.py:290
  83.5 0.7 copy.15
  84.1 0.7 copy.16
  84.8 0.7 copy.17
  85.4 0.6 copy.18
  86.1 0.7 copy.19
Async XLA Ops:
  0.6 0.9 %copy-start = (bf16[256,256]{1,0:T(8,128)(2,1)S(1)}, bf16[256,256]{1,0:T(8,128)(2,1)}, u32[]{:S(2)}) copy-start(bf16[256,256]{1,0:T(8,128)(2,1)} %b_ref.1) | copy-start | bytes 393220
  1.5 0.9 %copy-start.1 = (f32[256,128]{1,0:T(8,128)S(1)}, f32[256,128]{1,0:T(8,128)}, u32[]{:S(2)}) copy-start(f32[256,128]{1,0:T(8,128)} %fm_ref.1) | copy-start | bytes 393220
  2.4 0.9 %copy-start.2 = (f32[256,128]{1,0:T(8,128)S(1)}, f32[256,128]{1,0:T(8,128)}, u32[]{:S(2)}) copy-start(f32[256,128]{1,0:T(8,128)} %sm_ref.1) | copy-start | bytes 393220
  3.3 0.9 %copy-start.3 = (f32[256,128]{1,0:T(8,128)S(1)}, f32[256,128]{1,0:T(8,128)}, u32[]{:S(2)}) copy-start(f32[256,128]{1,0:T(8,128)} %ma_ref.1) | copy-start | bytes 393220
  4.3 0.8 copy-start.4

commit v2 on v0

v2 whole, which is shorter than its diff:
```python
import jax
import jax.numpy as jnp
from jax import lax
from jax.experimental import pallas as pl
from jax.experimental.pallas import tpu as pltpu
from jax.sharding import PartitionSpec as P

STEP = 10
BETA_ONE = 0.9
BETA_TWO = 0.95
EPSILON = 1e-08
LEARN = 0.01
DECAY = 0.1

MESH = pl.DeviceIdType.MESH
F32 = jnp.float32
BF16 = jnp.bfloat16

Z_STEPS = (4, 3)
DELTAS = (4, 3, -3, 2, -2, 1, -1, 0)
HOME = DELTAS.index(0)


def kernel(
    g_ref, b_ref, fm_ref, sm_ref,
    rot_ref, near_ref, dist_ref,
    fm, sm, rot, near, dist, give, stage, wide, tall, acc, part_out, part_in, turned,
    own, core_out, core_in, ring_out, ring_in, last_out, last_in,
    l_s, w_s, y_s, y_r, x_s, x_r, g_s, g_r, z_s, z_r, gc_s, gc_r, p_s, p_r, tc_s, tc_r, r_s, r_r, f_s, f_r,
):
    row, col = lax.axis_index("row"), lax.axis_index("col")
    z, yh, c = row // 4, (row // 2) % 2, row % 2
    yl, x = col // 8, col % 8
    h = yl % 2
    mate = yl + 1 - 2 * h
    far = 1 - yh
    here = yl * 8 + x

    def at(z_, yh_, c_, yl_, x_):
        return (z_ * 4 + yh_ * 2 + c_, yl_ * 8 + x_)

    right, left = at(z, yh, c, yl, (x + 1) % 8), at(z, yh, c, yl, (x + 7) % 8)
    right2, left2 = at(z, yh, c, yl, (x + 2) % 8), at(z, yh, c, yl, (x + 6) % 8)
    above, below = at((z + 1) % 8, yh, c, yl, x), at((z + 7) % 8, yh, c, yl, x)
    above2, below2 = at((z + 2) % 8, yh, c, yl, x), at((z + 6) % 8, yh, c, yl, x)
    twin = at(z, yh, 1 - c, yl, x)
    pair = at(z, yh, c, mate, x)
    two_off = at(z, yh, c, (yl + 2) % 4, x)
    mirror = at(z, yh, c, 3 - yl, x)
    across = at(z, far, c, yl, x)
    across_pair = at(z, far, c, mate, x)

    mine = pl.ds(pl.multiple_of(h * 128, 128), 128)
    other = pl.ds(pl.multiple_of((1 - h) * 128, 128), 128)
    loads = [
        pltpu.make_async_copy(src, dst, l_s.at[i])
        for i, (src, dst) in enumerate((
            (b_ref.at[:, mine], wide.at[here]),
            (b_ref.at[:, other], stage),
            (g_ref.at[mine, :], tall.at[z, c, yh, 0]),
            (g_ref.at[other, :], give),
            (fm_ref, fm.at[0]), (sm_ref, sm.at[0]),
        ))
    ]
    for load in loads:
        load.start()
    barrier = pltpu.get_barrier_semaphore()
    peers = [right, left, right2, left2, above, below, above2, below2, twin, pair, two_off, mirror, across, across_pair]
    for peer in peers:
        pl.semaphore_signal(barrier, inc=1, device_id=peer, device_id_type=MESH)

    for load in loads[:4]:
        load.wait()
    pl.semaphore_wait(barrier, len(peers))

    waits = []

    def copy(src, dst, send, recv, to, later=True):
        made = pltpu.make_async_remote_copy(
            src_ref=src, dst_ref=dst, send_sem=send, recv_sem=recv, device_id=to, device_id_type=MESH
        )
        made.start()
        if later:
            waits.append(made)

    def arrived(dst, send, recv, frm):
        pltpu.make_async_remote_copy(
            src_ref=dst, dst_ref=dst, send_sem=send, recv_sem=recv, device_id=frm, device_id_type=MESH
        ).wait_recv()

    inner = ((yl + 1) // 2) % 2
    two, three = (yl + 2) % 4, 3 - yl
    lines = (yl, mate, inner * three + (1 - inner) * two, inner * two + (1 - inner) * three)
    came_by = (None, 0, inner + 1, 2 - inner)

    def x_slot(d, way, s):
        return wide.at[lines[d] * 8 + (x + 8 + (-1, 1)[way] * s) % 8]

    def x_half(d, way):
        return wide.at[lines[d] * 8 + (x + 4) % 8, pl.ds(way * 128, 128)]

    def x_step(d, s):
        for way, to in ((0, right), (1, left)):
            slot = x_slot(d, way, s)
            if s:
                arrived(slot, x_s.at[0], x_r.at[way, d, s - 1], to)
            if s == 3:
                slot = slot.at[pl.ds(way * 128, 128)]
            copy(slot, slot, x_s.at[0], x_r.at[way, d, s], to, later=False)

    def x_first():
        slot = x_slot(0, 0, 0)
        for s, ways in ((0, (right, left)), (1, (right2, left2))):
            for way in (0, 1):
                copy(slot, slot, x_s.at[0], x_r.at[way, 0, s], ways[way], later=False)

    def x_second():
        for way, one, two_on in ((0, right, right2), (1, left, left2)):
            slot = x_slot(0, way, 2)
            arrived(slot, x_s.at[0], x_r.at[way, 0, 1], one)
            copy(slot, slot, x_s.at[0], x_r.at[way, 0, 2], one, later=False)
            part = slot.at[pl.ds(way * 128, 128)]
            copy(part, part, x_s.at[0], x_r.at[way, 0, 3], two_on, later=False)

    def x_last(d):
        for way, one in ((0, right), (1, left)):
            if d == 0:
                arrived(x_slot(0, way, 1), x_s.at[0], x_r.at[way, 0, 0], one)
                arrived(x_slot(0, way, 3), x_s.at[0], x_r.at[way, 0, 2], one)
            arrived(x_half(d, way), x_s.at[0], x_r.at[way, d, 3], one)

    def y_step(d):
        arrived(wide.at[lines[d] * 8 + x], y_s.at[0], y_r.at[came_by[d]], pair)
        x_step(d, 0)

    halves = (yh, far)

    def to_twin(a, way, s):
        sign = (-1, 1)[way]
        slot = tall.at[(z + 8 + sign * s) % 8, c, halves[a]]
        copy(slot, slot, gc_s.at[0], gc_r.at[way, a, s], twin, later=False)

    def twin_arrived(a, way, s):
        sign = (-1, 1)[way]
        slot = tall.at[(z + 8 + sign * s) % 8, 1 - c, halves[a]]
        arrived(slot, gc_s.at[0], gc_r.at[way, a, s], twin)

    def z_step(s):
        for way, sign, to in ((0, -1, above), (1, 1, below)):
            if s > Z_STEPS[way]:
                continue
            slot = tall.at[(z + 8 + sign * s) % 8, c, yh]
            if s:
                arrived(slot, z_s.at[0], z_r.at[way, 0, s - 1], to)
            if s < Z_STEPS[way]:
                copy(slot, slot, z_s.at[0], z_r.at[way, 0, s], to, later=False)
            if s or way == 0:
                to_twin(0, way, s)

    def far_first():
        slot = tall.at[z, c, far]
        for s, ways in ((1, (above2, below2)), (0, (above, below))):
            for way in (0, 1):
                copy(slot, slot, z_s.at[0], z_r.at[way, 1, s], ways[way], later=False)
        to_twin(1, 0, 0)

    def far_second():
        for way, sign, one, two_on in ((0, -1, above, above2), (1, 1, below, below2)):
            slot = tall.at[(z + 8 + sign * 2) % 8, c, far]
            arrived(slot, z_s.at[0], z_r.at[way, 1, 1], one)
            copy(slot.at[way], slot.at[way], z_s.at[0], z_r.at[way, 1, 3], two_on, later=False)
            copy(slot, slot, z_s.at[0], z_r.at[way, 1, 2], one, later=False)
        for s in (2, 1):
            for way, sign, one in ((0, -1, above), (1, 1, below)):
                if s == 1:
                    arrived(tall.at[(z + 8 + sign) % 8, c, far], z_s.at[0], z_r.at[way, 1, 0], one)
                to_twin(1, way, s)

    def far_third():
        for way, sign, one in ((0, -1, above), (1, 1, below)):
            arrived(tall.at[(z + 8 + sign * 3) % 8, c, far], z_s.at[0], z_r.at[way, 1, 2], one)
            to_twin(1, way, 3)
        for way, one in ((0, above), (1, below)):
            arrived(tall.at[(z + 4) % 8, c, far, way], z_s.at[0], z_r.at[way, 1, 3], one)
        to_twin(1, 0, 4)

    x_first()
    copy(give, tall.at[z, c, yh, 1], g_s.at[1], g_r.at[1], pair)
    copy(stage, wide.at[here], y_s.at[0], y_r.at[0], pair)
    copy(tall.at[z, c, yh, 0], tall.at[z, c, yh, 0], g_s.at[0], g_r.at[0], across)
    copy(give, tall.at[z, c, yh, 1], g_s.at[2], g_r.at[2], across_pair)
    copy(stage, wide.at[here], y_s.at[2], y_r.at[2], mirror)
    copy(wide.at[here], wide.at[here], y_s.at[1], y_r.at[1], two_off)

    arrived(tall.at[z, c, yh, 1], g_s.at[1], g_r.at[1], pair)
    z_step(0)
    y_step(1)
    x_second()
    y_step(2)
    z_step(1)
    x_step(1, 1)
    y_step(3)
    arrived(tall.at[z, c, far, 0], g_s.at[0], g_r.at[0], across)
    arrived(tall.at[z, c, far, 1], g_s.at[2], g_r.at[2], across_pair)
    far_first()
    for load in loads[4:]:
        load.wait()
    copy(fm.at[0], fm.at[1], p_s.at[1], p_r.at[1], pair)
    copy(sm.at[0], sm.at[1], p_s.at[2], p_r.at[2], pair)
    x_step(2, 1)
    x_step(1, 2)
    x_step(3, 1)
    z_step(2)
    x_step(2, 2)
    x_step(1, 3)
    x_step(3, 2)
    z_step(3)
    far_second()
    x_step(2, 3)
    x_step(3, 3)
    z_step(4)
    far_third()
    for d in range(4):
        x_last(d)

    places = ((0, 0), (0, 1), (1, 1), (0, 2), (1, 2), (0, 3), (1, 3), (0, 4))
    for i, (way, s) in enumerate(places):
        for a in (0, 1):
            twin_arrived(a, way, s)
        there = (z + 8 + (-1, 1)[way] * s) % 8
        lhs = jnp.concatenate([wide[there * 4 + k] for k in range(4)], axis=1)
        rhs = jnp.concatenate(
            [
                jnp.concatenate([tall[there, k % 2, k // 2, e] for k in range(4)], axis=0)
                for e in (0, 1)
            ],
            axis=1,
        )
        term = jnp.dot(lhs, rhs, preferred_element_type=F32)
        acc[...] = term if i == 0 else acc[...] + term
    part_out[0] = acc[:, 0:128].astype(BF16)
    part_out[1] = acc[:, 128:256].astype(BF16)
    copy(part_out, part_in, p_s.at[0], p_r.at[0], pair)

    writes = [
        pltpu.make_async_copy(src, dst, w_s.at[i])
        for i, (src, dst) in enumerate(((rot, rot_ref), (near, near_ref), (dist, dist_ref)))
    ]

    def turn(e):
        rotated = acc[:, e * 128 : e * 128 + 128] + part_in[1 - e].astype(F32)
        if e == 0:
            rot[...] = rotated
            writes[0].start()
        new_first = BETA_ONE * fm[e] + (1.0 - BETA_ONE) * rotated
        new_second = BETA_TWO * sm[e] + (1.0 - BETA_TWO) * rotated * rotated
        corr_one = 1.0 - BETA_ONE**STEP
        corr_two = 1.0 - BETA_TWO**STEP
        direction = new_first / corr_one / (jnp.sqrt(new_second / corr_two) + EPSILON)
        turned[e] = direction.T.astype(BF16)

    arrived(fm.at[1], p_s.at[1], p_r.at[1], pair)
    arrived(sm.at[1], p_s.at[2], p_r.at[2], pair)
    arrived(part_in, p_s.at[0], p_r.at[0], pair)

    def terms(e, first, last):
        lhs = turned[e]
        for i in range(first, last):
            base = ((z + 8 + DELTAS[i]) % 8) * 4
            for half in (0, 1):
                rhs = jnp.concatenate([wide[base + half * 2 + c], wide[base + half * 2 + 1 - c]], axis=1)
                term = jnp.dot(lhs, rhs, preferred_element_type=F32)
                own[e, i, half] = term[:, 0:128]
                core_out[e, i, half] = term[:, 128:256].astype(BF16)
            copy(core_out.at[e, i], core_in.at[e, i], tc_s.at[0], tc_r.at[e, i], twin, later=False)

    def from_twin(e, i):
        arrived(core_in.at[e, i], tc_s.at[0], tc_r.at[e, i], twin)

    def stride(e, kind):
        for way in (0, 1):
            to = ((above, below), (above2, below2), (above, below), (above, below))[kind][way]
            i = DELTAS.index(((3, -3), (4, 4), (1, -1), (2, -2))[kind][way])
            if kind == 1:
                total = own[e, i, way] + core_in[e, i, way].astype(F32)
                sent, there = ring_out.at[way, e, 1, way], ring_in.at[way, e, 1, way]
            else:
                total = own[e, i] + core_in[e, i].astype(F32)
                sent, there = ring_out.at[way, e, kind], ring_in.at[way, e, kind]
            if kind == 3:
                arrived(ring_in.at[way, e, 0], r_s.at[0], r_r.at[way, e, 0], to)
                total += ring_in[way, e, 0].astype(F32)
                arrived(ring_in.at[way, e, 1, way], r_s.at[0], r_r.at[way, e, 1], to)
                own[e, i] = total
                own[e, i, way] = own[e, i, way] + ring_in[way, e, 1, way].astype(F32)
                total = own[e, i]
            if kind == 2:
                arrived(ring_in.at[way, e, 3], r_s.at[0], r_r.at[way, e, 3], to)
                total += ring_in[way, e, 3].astype(F32)
            sent[...] = total.astype(BF16)
            copy(sent, there, r_s.at[0], r_r.at[way, e, kind], to, later=False)

    def z_sum(e):
        from_twin(e, HOME)
        total = own[e, HOME] + core_in[e, HOME].astype(F32)
        for way in (0, 1):
            arrived(ring_in.at[way, e, 2], r_s.at[0], r_r.at[way, e, 2], above)
            total += ring_in[way, e, 2].astype(F32)
        own[e, HOME] = total
        last_out[e] = total.astype(BF16)

    turn(0)
    terms(0, 0, 3)
    turn(1)
    terms(1, 0, 3)
    for i in range(3):
        from_twin(0, i)
    stride(0, 0)
    stride(0, 1)
    terms(0, 3, 8)
    for i in range(3):
        from_twin(1, i)
    stride(1, 0)
    stride(1, 1)
    terms(1, 3, 8)
    for i in range(3, 7):
        from_twin(0, i)
    for i in range(3, 7):
        from_twin(1, i)
    stride(0, 3)
    stride(1, 3)
    stride(0, 2)
    stride(1, 2)
    z_sum(0)
    copy(last_out.at[0, far], last_in.at[0], f_s.at[0], f_r.at[0], across)
    z_sum(1)
    copy(last_out.at[1, far], last_in.at[2], f_s.at[2], f_r.at[2], across_pair)
    copy(last_out.at[1, yh], last_in.at[1], f_s.at[1], f_r.at[1], pair)

    pltpu.make_async_copy(wide.at[pl.ds(0, 28)], wide.at[pl.ds(0, 28)], x_s.at[0]).wait()
    pltpu.make_async_copy(tall.at[pl.ds(0, 7), 0], tall.at[pl.ds(0, 7), 0], z_s.at[0]).wait()
    pltpu.make_async_copy(tall.at[:, 0], tall.at[:, 0], gc_s.at[0]).wait()
    pltpu.make_async_copy(core_out, core_out, tc_s.at[0]).wait()
    pltpu.make_async_copy(ring_out.at[:, 1, pl.ds(1, 3)], ring_out.at[:, 1, pl.ds(1, 3)], r_s.at[0]).wait()
    pltpu.make_async_copy(ring_out.at[0], ring_out.at[0], r_s.at[0]).wait()
    for made in waits[:-3]:
        made.wait_send()

    near[mine, :] = own[0, HOME, yh].T
    arrived(last_in.at[1], f_s.at[1], f_r.at[1], pair)
    near[other, :] = last_in[1].astype(F32).T
    writes[1].start()
    arrived(last_in.at[2], f_s.at[2], f_r.at[2], across_pair)
    dist[other, :] = last_in[2].astype(F32).T
    arrived(last_in.at[0], f_s.at[0], f_r.at[0], across)
    dist[mine, :] = last_in[0].astype(F32).T
    writes[2].start()
    for made in waits[-3:]:
        made.wait_send()
    for made in writes:
        made.wait()


def shards(grad, basis_t, first_moment, second_moment, master):
    block = jax.ShapeDtypeStruct(grad.shape, F32)
    dma = pltpu.SemaphoreType.DMA
    rotated, near, dist = pl.pallas_call(
        kernel,
        out_shape=(block, block, block),
        in_specs=[pl.BlockSpec(memory_space=pltpu.HBM)] * 4,
        out_specs=tuple([pl.BlockSpec(memory_space=pltpu.HBM)] * 3),
        scratch_shapes=[
            pltpu.VMEM((2, 256, 128), F32),
            pltpu.VMEM((2, 256, 128), F32),
            pltpu.VMEM((256, 128), F32),
            pltpu.VMEM((256, 128), F32),
            pltpu.VMEM((256, 128), F32),
            pltpu.VMEM((128, 128), BF16),
            pltpu.VMEM((256, 128), BF16),
            pltpu.VMEM((32, 256, 128), BF16),
            pltpu.VMEM((8, 2, 2, 2, 128, 128), BF16),
            pltpu.VMEM((256, 256), F32),
            pltpu.VMEM((2, 256, 128), BF16),
            pltpu.VMEM((2, 256, 128), BF16),
            pltpu.VMEM((2, 128, 256), BF16),
            pltpu.VMEM((2, 8, 2, 128, 128), F32),
            pltpu.VMEM((2, 8, 2, 128, 128), BF16),
            pltpu.VMEM((2, 8, 2, 128, 128), BF16),
            pltpu.VMEM((2, 2, 4, 2, 128, 128), BF16),
            pltpu.VMEM((2, 2, 4, 2, 128, 128), BF16),
            pltpu.VMEM((2, 2, 128, 128), BF16),
            pltpu.VMEM((3, 128, 128), BF16),
            dma((6,)), dma((3,)),
            dma((3,)), dma((3,)),
            dma((1,)), dma((2, 4, 4)),
            dma((3,)), dma((3,)),
            dma((1,)), dma((2, 2, 4)),
            dma((1,)), dma((2, 2, 5)),
            dma((3,)), dma((3,)),
            dma((1,)), dma((2, 8)),
            dma((1,)), dma((2, 2, 4)),
            dma((3,)), dma((3,)),
        ],
        compiler_params=pltpu.CompilerParams(
            collective_id=0, has_side_effects=True, vmem_limit_bytes=60 * 2**20
        ),
        cost_estimate=pl.CostEstimate(flops=2 * 2 * 256 * 8192 * 128, bytes_accessed=2**20, transcendentals=0),
    )(grad, basis_t, first_moment, second_moment)
    new_first = BETA_ONE * first_moment + (1.0 - BETA_ONE) * rotated
    new_second = BETA_TWO * second_moment + (1.0 - BETA_TWO) * rotated * rotated
    rotated_back = near + dist
    new_master = master * (1.0 - LEARN * DECAY) - LEARN * rotated_back
    return (new_first, new_second, new_master, new_master.astype(BF16), rotated_back)


def solution(mesh):
    placed = tuple([P("row", "col")] * 5)
    return jax.shard_map(shards, mesh=mesh, in_specs=placed, out_specs=placed, check_vma=False)
```

time: 425 us -> 81.2 us (0.19)
  waiting for transfers between devices: 396 us -> 0 us
  Pallas kernels: 0 us -> 78.1 us
  between operations: 13.8 us -> 0.69 us
  matrix products: 6.34 us -> 0 us
    all_gather x2 -> x0, waiting for transfers between devices: 237 us -> none  [the longest x1 120 us: shards(): wide = lax.all_gather(basis_t, 'col', axis=1, tiled=True)]
    reduce_scatter x1 -> x0, waiting for transfers between devices: 157 us -> none  [shards(): lax.psum_scatter(terms.astype(jnp.bfloat16), 'row', scatter_dimension=0,...]
    pallas_call x0 -> x1, Pallas kernels: none -> 78.1 us  [shards(): pl.pallas_call(kernel, out_shape=(block, block, block), in_specs=[pl.Bloc...]
    dot_general x2 -> x0, matrix products: 6.34 us -> none  [the longest x1 4.21 us: shards(): rotated = jnp.dot(wide, tall, preferred_element_type=jnp.float32)]
  transfers between devices with their start and end apart: 3 -> 0, of which waited for: 3 -> 0; matrix products, arithmetic and copies ran while one was open for 0% -> 0% of each run, Pallas kernels for 0% -> 0%
where the time goes in v2:
time: 81.2 us; the launch traced here: 80.7 us
  Pallas kernels  78.1 us (96%)
  other arithmetic  1.86 us (2%)
    pallas_call x1, Pallas kernels, shards(): pl.pallas_call(kernel, out_shape=(block, block, block), in_specs=[pl.Bloc...  78.1 us
    add x1, other arithmetic, shards(): new_second = BETA_TWO * second_moment + (1.0 - BETA_TWO) * rotated * rotated  1.86 us

profile of v2, /device:TPU:1, one launch (start us, length us, event | category | flops | bytes accessed | tf_op | source)
XLA Modules:
  0.0 80.7 jit_solution(1165996779575977608)
XLA Ops:
  0.6 0.0 copy-start.1
  0.6 0.0 copy-start
  0.7 0.0 copy-start.2
  0.7 78.1 %shard_map.92 = (f32[256,128]{1,0:T(8,128)}, f32[256,128]{1,0:T(8,128)}, f32[256,128]{1,0:T(8,128)}) custom-call(bf16[256,128]{1,0:T(8,128)(2,1)} %g_ref.1, bf16[256,256]{1,0:T(8,128)(2,1)} %b_ref.1, f32[256,128]{1,0:T(8,128)} %fm_ref.1, f32[256,128]{1,0:T(8,128)} %sm_ref.1), custom_call_target="tpu_custom_call" | custom-call | flops 1073741824 | bytes 1048576 | tf_op jit(solution)/shard_map/pallas_call | solution.py:367
  78.8 0.0 copy-done.1
  78.8 0.0 copy-done
  78.8 0.0 copy-done.2
  78.8 1.9 %fusion = (f32[256,128]{1,0:T(8,128)}, f32[256,128]{1,0:T(8,128)}, bf16[256,128]{1,0:T(8,128)(2,1)}, f32[256,128]{1,0:T(8,128)}, f32[256,128]{1,0:T(8,128)}) fusion(f32[256,128]{1,0:T(8,128)} %get-tuple-element.8, f32[256,128]{1,0:T(8,128)S(1)} %copy-done.1, f32[256,128]{1,0:T(8,128)S(1)} %copy-done, f32[256,128]{1,0:T(8,128)} %get-tuple-element.9, ...), kind=kLoop, calls=%fused_computation.1 | loop fusion | flops 393216 | bytes 1376256 | tf_op jit(solution)/shard_map/add | solution.py:410
Async XLA Ops:
  0.6 78.2 %copy-start.1 = (f32[256,128]{1,0:T(8,128)S(1)}, f32[256,128]{1,0:T(8,128)}, u32[]{:S(2)}) copy-start(f32[256,128]{1,0:T(8,128)} %sm_ref.1) | copy-start | bytes 393220
  0.6 78.2 %copy-start = (f32[256,128]{1,0:T(8,128)S(1)}, f32[256,128]{1,0:T(8,128)}, u32[]{:S(2)}) copy-start(f32[256,128]{1,0:T(8,128)} %fm_ref.1) | copy-start | bytes 393220
  0.7 78.2 %copy-start.2 = (f32[256,128]{1,0:T(8,128)S(1)}, f32[256,128]{1,0:T(8,128)}, u32[]{:S(2)}) copy-start(f32[256,128]{1,0:T(8,128)} %param.9) | copy-start | bytes 393220

commit v3 on v2

--- a/solution.py
+++ b/solution.py
@@ -187,13 +187,13 @@
     x_first()
     copy(give, tall.at[z, c, yh, 1], g_s.at[1], g_r.at[1], pair)
     copy(stage, wide.at[here], y_s.at[0], y_r.at[0], pair)
+    copy(stage, wide.at[here], y_s.at[2], y_r.at[2], mirror)
+    copy(wide.at[here], wide.at[here], y_s.at[1], y_r.at[1], two_off)
+
+    arrived(tall.at[z, c, yh, 1], g_s.at[1], g_r.at[1], pair)
+    z_step(0)
     copy(tall.at[z, c, yh, 0], tall.at[z, c, yh, 0], g_s.at[0], g_r.at[0], across)
     copy(give, tall.at[z, c, yh, 1], g_s.at[2], g_r.at[2], across_pair)
-    copy(stage, wide.at[here], y_s.at[2], y_r.at[2], mirror)
-    copy(wide.at[here], wide.at[here], y_s.at[1], y_r.at[1], two_off)
-
-    arrived(tall.at[z, c, yh, 1], g_s.at[1], g_r.at[1], pair)
-    z_step(0)
     y_step(1)
     x_second()
     y_step(2)
@@ -208,39 +208,47 @@
     copy(fm.at[0], fm.at[1], p_s.at[1], p_r.at[1], pair)
     copy(sm.at[0], sm.at[1], p_s.at[2], p_r.at[2], pair)
     x_step(2, 1)
+    z_step(2)
     x_step(1, 2)
     x_step(3, 1)
-    z_step(2)
     x_step(2, 2)
+    far_second()
+    z_step(3)
     x_step(1, 3)
     x_step(3, 2)
-    z_step(3)
-    far_second()
     x_step(2, 3)
-    x_step(3, 3)
     z_step(4)
     far_third()
-    for d in range(4):
-        x_last(d)
-
-    places = ((0, 0), (0, 1), (1, 1), (0, 2), (1, 2), (0, 3), (1, 3), (0, 4))
-    for i, (way, s) in enumerate(places):
+    x_step(3, 3)
+    x_last(0)
+    for s in range(5):
         for a in (0, 1):
-            twin_arrived(a, way, s)
-        there = (z + 8 + (-1, 1)[way] * s) % 8
-        lhs = jnp.concatenate([wide[there * 4 + k] for k in range(4)], axis=1)
+            for way in (0, 1):
+                if way == 0 or s in (1, 2, 3):
+                    twin_arrived(a, way, s)
+
+    for delta in (0, 1, -1, 2, -2, 3, -3, 4):
+        if delta == 4:
+            for d in (1, 2, 3):
+                x_last(d)
+        there = (x + 8 + delta) % 8
+        lhs = jnp.concatenate([wide[line * 8 + there] for line in range(4)], axis=1)
         rhs = jnp.concatenate(
             [
-                jnp.concatenate([tall[there, k % 2, k // 2, e] for k in range(4)], axis=0)
+                jnp.concatenate(
+                    [tall[line * 2 + there // 4, there % 2, (there // 2) % 2, e] for line in range(4)],
+                    axis=0,
+                )
                 for e in (0, 1)
             ],
             axis=1,
         )
         term = jnp.dot(lhs, rhs, preferred_element_type=F32)
-        acc[...] = term if i == 0 else acc[...] + term
+        acc[...] = term if delta == 0 else acc[...] + term
     part_out[0] = acc[:, 0:128].astype(BF16)
+    copy(part_out.at[0], part_in.at[0], p_s.at[0], p_r.at[0], pair)
     part_out[1] = acc[:, 128:256].astype(BF16)
-    copy(part_out, part_in, p_s.at[0], p_r.at[0], pair)
+    copy(part_out.at[1], part_in.at[1], p_s.at[3], p_r.at[3], pair)
 
     writes = [
         pltpu.make_async_copy(src, dst, w_s.at[i])
@@ -261,7 +269,7 @@
 
     arrived(fm.at[1], p_s.at[1], p_r.at[1], pair)
     arrived(sm.at[1], p_s.at[2], p_r.at[2], pair)
-    arrived(part_in, p_s.at[0], p_r.at[0], pair)
+    arrived(part_in.at[0], p_s.at[0], p_r.at[0], pair)
 
     def terms(e, first, last):
         lhs = turned[e]
@@ -309,33 +317,34 @@
         own[e, HOME] = total
         last_out[e] = total.astype(BF16)
 
+    turn(1)
+    terms(1, 0, 3)
+    arrived(part_in.at[1], p_s.at[3], p_r.at[3], pair)
     turn(0)
     terms(0, 0, 3)
-    turn(1)
-    terms(1, 0, 3)
+    for i in range(3):
+        from_twin(1, i)
+    stride(1, 0)
+    stride(1, 1)
+    terms(1, 3, 8)
     for i in range(3):
         from_twin(0, i)
     stride(0, 0)
     stride(0, 1)
     terms(0, 3, 8)
-    for i in range(3):
+    for i in range(3, 7):
         from_twin(1, i)
-    stride(1, 0)
-    stride(1, 1)
-    terms(1, 3, 8)
     for i in range(3, 7):
         from_twin(0, i)
-    for i in range(3, 7):
-        from_twin(1, i)
+    stride(1, 3)
     stride(0, 3)
-    stride(1, 3)
+    stride(1, 2)
     stride(0, 2)
-    stride(1, 2)
-    z_sum(0)
-    copy(last_out.at[0, far], last_in.at[0], f_s.at[0], f_r.at[0], across)
     z_sum(1)
     copy(last_out.at[1, far], last_in.at[2], f_s.at[2], f_r.at[2], across_pair)
     copy(last_out.at[1, yh], last_in.at[1], f_s.at[1], f_r.at[1], pair)
+    z_sum(0)
+    copy(last_out.at[0, far], last_in.at[0], f_s.at[0], f_r.at[0], across)
 
     pltpu.make_async_copy(wide.at[pl.ds(0, 28)], wide.at[pl.ds(0, 28)], x_s.at[0]).wait()
     pltpu.make_async_copy(tall.at[pl.ds(0, 7), 0], tall.at[pl.ds(0, 7), 0], z_s.at[0]).wait()
@@ -396,7 +405,7 @@
             dma((3,)), dma((3,)),
             dma((1,)), dma((2, 2, 4)),
             dma((1,)), dma((2, 2, 5)),
-            dma((3,)), dma((3,)),
+            dma((4,)), dma((4,)),
             dma((1,)), dma((2, 8)),
             dma((1,)), dma((2, 2, 4)),
             dma((3,)), dma((3,)),

time: 81.2 us -> 79.2 us (0.975)
  Pallas kernels: 78.1 us -> 76.5 us
    pallas_call x1, Pallas kernels: 78.1 us -> 76.5 us  [shards(): pl.pallas_call(kernel, out_shape=(block, block, block), in_specs=[pl.Bloc...]
where the time goes in v3:
time: 79.2 us; the launch traced here: 79.1 us
  Pallas kernels  76.5 us (97%)
  other arithmetic  1.86 us (2%)
    pallas_call x1, Pallas kernels, shards(): pl.pallas_call(kernel, out_shape=(block, block, block), in_specs=[pl.Bloc...  76.5 us
    add x1, other arithmetic, shards(): new_second = BETA_TWO * second_moment + (1.0 - BETA_TWO) * rotated * rotated  1.86 us

profile of v3, /device:TPU:1, one launch (start us, length us, event | category | flops | bytes accessed | tf_op | source)
XLA Modules:
  0.0 79.1 jit_solution(4669320400267488984)
XLA Ops:
  0.6 0.0 copy-start.1
  0.6 0.0 copy-start
  0.7 0.0 copy-start.2
  0.7 76.5 %shard_map.92 = (f32[256,128]{1,0:T(8,128)}, f32[256,128]{1,0:T(8,128)}, f32[256,128]{1,0:T(8,128)}) custom-call(bf16[256,128]{1,0:T(8,128)(2,1)} %g_ref.1, bf16[256,256]{1,0:T(8,128)(2,1)} %b_ref.1, f32[256,128]{1,0:T(8,128)} %fm_ref.1, f32[256,128]{1,0:T(8,128)} %sm_ref.1), custom_call_target="tpu_custom_call" | custom-call | flops 1073741824 | bytes 1048576 | tf_op jit(solution)/shard_map/pallas_call | solution.py:376
  77.2 0.0 copy-done.1
  77.2 0.0 copy-done
  77.2 0.0 copy-done.2
  77.2 1.9 %fusion = (f32[256,128]{1,0:T(8,128)}, f32[256,128]{1,0:T(8,128)}, bf16[256,128]{1,0:T(8,128)(2,1)}, f32[256,128]{1,0:T(8,128)}, f32[256,128]{1,0:T(8,128)}) fusion(f32[256,128]{1,0:T(8,128)} %get-tuple-element.8, f32[256,128]{1,0:T(8,128)S(1)} %copy-done.1, f32[256,128]{1,0:T(8,128)S(1)} %copy-done, f32[256,128]{1,0:T(8,128)} %get-tuple-element.9, ...), kind=kLoop, calls=%fused_computation.1 | loop fusion | flops 393216 | bytes 1376256 | tf_op jit(solution)/shard_map/add | solution.py:419
Async XLA Ops:
  0.6 76.5 %copy-start.1 = (f32[256,128]{1,0:T(8,128)S(1)}, f32[256,128]{1,0:T(8,128)}, u32[]{:S(2)}) copy-start(f32[256,128]{1,0:T(8,128)} %sm_ref.1) | copy-start | bytes 393220
  0.6 76.5 %copy-start = (f32[256,128]{1,0:T(8,128)S(1)}, f32[256,128]{1,0:T(8,128)}, u32[]{:S(2)}) copy-start(f32[256,128]{1,0:T(8,128)} %fm_ref.1) | copy-start | bytes 393220
  0.7 76.5 %copy-start.2 = (f32[256,128]{1,0:T(8,128)S(1)}, f32[256,128]{1,0:T(8,128)}, u32[]{:S(2)}) copy-start(f32[256,128]{1,0:T(8,128)} %param.9) | copy-start | bytes 393220

commit v4 on v3

--- a/solution.py
+++ b/solution.py
@@ -360,9 +360,9 @@
     near[other, :] = last_in[1].astype(F32).T
     writes[1].start()
     arrived(last_in.at[2], f_s.at[2], f_r.at[2], across_pair)
-    dist[other, :] = last_in[2].astype(F32).T
+    dist[other, :] = last_in[2].astype(F32).T.astype(BF16)
     arrived(last_in.at[0], f_s.at[0], f_r.at[0], across)
-    dist[mine, :] = last_in[0].astype(F32).T
+    dist[mine, :] = last_in[0].astype(F32).T.astype(BF16)
     writes[2].start()
     for made in waits[-3:]:
         made.wait_send()
@@ -375,7 +375,7 @@
     dma = pltpu.SemaphoreType.DMA
     rotated, near, dist = pl.pallas_call(
         kernel,
-        out_shape=(block, block, block),
+        out_shape=(block, block, jax.ShapeDtypeStruct(grad.shape, BF16)),
         in_specs=[pl.BlockSpec(memory_space=pltpu.HBM)] * 4,
         out_specs=tuple([pl.BlockSpec(memory_space=pltpu.HBM)] * 3),
         scratch_shapes=[
@@ -383,7 +383,7 @@
             pltpu.VMEM((2, 256, 128), F32),
             pltpu.VMEM((256, 128), F32),
             pltpu.VMEM((256, 128), F32),
-            pltpu.VMEM((256, 128), F32),
+            pltpu.VMEM((256, 128), BF16),
             pltpu.VMEM((128, 128), BF16),
             pltpu.VMEM((256, 128), BF16),
             pltpu.VMEM((32, 256, 128), BF16),
@@ -417,7 +417,7 @@
     )(grad, basis_t, first_moment, second_moment)
     new_first = BETA_ONE * first_moment + (1.0 - BETA_ONE) * rotated
     new_second = BETA_TWO * second_moment + (1.0 - BETA_TWO) * rotated * rotated
-    rotated_back = near + dist
+    rotated_back = near + dist.astype(F32)
     new_master = master * (1.0 - LEARN * DECAY) - LEARN * rotated_back
     return (new_first, new_second, new_master, new_master.astype(BF16), rotated_back)
 

time: 79.2 us -> 79.1 us (level)
  no operation moved by 1% of the time
where the time goes in v4:
time: 79.1 us; the launch traced here: 78.9 us
  Pallas kernels  76.4 us (97%)
  other arithmetic  1.8 us (2%)
    pallas_call x1, Pallas kernels, shards(): pl.pallas_call(kernel, out_shape=(block, block, jax.ShapeDtypeStruct(grad...  76.4 us
    add x1, other arithmetic, shards(): new_second = BETA_TWO * second_moment + (1.0 - BETA_TWO) * rotated * rotated  1.8 us

profile of v4, /device:TPU:1, one launch (start us, length us, event | category | flops | bytes accessed | tf_op | source)
XLA Modules:
  0.0 78.9 jit_solution(15116281686059814318)
XLA Ops:
  0.6 0.0 copy-start.1
  0.6 0.0 copy-start
  0.7 0.0 copy-start.2
  0.7 76.4 %shard_map.92 = (f32[256,128]{1,0:T(8,128)}, f32[256,128]{1,0:T(8,128)}, bf16[256,128]{1,0:T(8,128)(2,1)}) custom-call(bf16[256,128]{1,0:T(8,128)(2,1)} %g_ref.1, bf16[256,256]{1,0:T(8,128)(2,1)} %b_ref.1, f32[256,128]{1,0:T(8,128)} %fm_ref.1, f32[256,128]{1,0:T(8,128)} %sm_ref.1), custom_call_target="tpu_custom_call" | custom-call | flops 1073741824 | bytes 1048576 | tf_op jit(solution)/shard_map/pallas_call | solution.py:376
  77.1 0.0 copy-done.1
  77.1 0.0 copy-done
  77.1 0.0 copy-done.2
  77.1 1.8 %fusion = (f32[256,128]{1,0:T(8,128)}, f32[256,128]{1,0:T(8,128)}, bf16[256,128]{1,0:T(8,128)(2,1)}, f32[256,128]{1,0:T(8,128)}, f32[256,128]{1,0:T(8,128)}) fusion(f32[256,128]{1,0:T(8,128)} %get-tuple-element.8, f32[256,128]{1,0:T(8,128)S(1)} %copy-done.1, f32[256,128]{1,0:T(8,128)S(1)} %copy-done, f32[256,128]{1,0:T(8,128)} %get-tuple-element.9, ...), kind=kLoop, calls=%fused_computation.1 | loop fusion | flops 425984 | bytes 1310720 | tf_op jit(solution)/shard_map/add | solution.py:419
Async XLA Ops:
  0.6 76.5 %copy-start.1 = (f32[256,128]{1,0:T(8,128)S(1)}, f32[256,128]{1,0:T(8,128)}, u32[]{:S(2)}) copy-start(f32[256,128]{1,0:T(8,128)} %sm_ref.1) | copy-start | bytes 393220
  0.6 76.5 %copy-start = (f32[256,128]{1,0:T(8,128)S(1)}, f32[256,128]{1,0:T(8,128)}, u32[]{:S(2)}) copy-start(f32[256,128]{1,0:T(8,128)} %fm_ref.1) | copy-start | bytes 393220
  0.7 76.5 %copy-start.2 = (f32[256,128]{1,0:T(8,128)S(1)}, f32[256,128]{1,0:T(8,128)}, u32[]{:S(2)}) copy-start(f32[256,128]{1,0:T(8,128)} %param.9) | copy-start | bytes 393220
